TPU v7x, 32 devices: a whole 2x2x4 slice. The times are simulated.
32 devices in a mesh: freq: 16 (over z, y, x), panel: 2 (over core).
Axes of the slice: x: 2, y: 2, z: 4, core: 2. Of those that a mesh axis runs over, the one named last changes fastest.
Arguments:
- shot_gathers: bfloat16 [64, 2048, 2048], P('freq', 'panel'), may hold values from -6 to 6
- aperture_blocks: int32 [32], replicated, may hold values from 8 to 16, as said below
- taper_index: int32 [32], replicated, may hold values from 0 to 3
Outputs:
- predicted: bfloat16 [64, 2048, 128], P('freq', 'panel')
Inputs may be any that keep to these rules, and one draw needn't show every extreme that they name: `aperture_blocks`: aperture of each frequency in blocks of 128 surface points, counted from the first point; the largest value occurs in every draw.
All inputs are finite; a program needn't handle non-finite values.
Results may differ from a plain program's by a relative error of at most 0.0076.
Values may be sent and summed in bfloat16 or wider, within the bound.
A program may use at most 128 MiB of HBM per device.

v0:
```python
import math
import jax
import jax.numpy as jnp
from jax import lax
from jax.sharding import PartitionSpec as P

SW = 128
BLOCK = 128
F_DEV = 2
TAPER = 64


def transform_tables(freq_total, time_total):
    bins = jnp.arange(freq_total, dtype=jnp.int32) + 1
    times = jnp.arange(time_total, dtype=jnp.int32)
    phase = bins[:, None] * times[None, :] % time_total
    angle = phase.astype(jnp.float32) * (2.0 * math.pi / time_total)
    scale = 1.0 / math.sqrt(time_total)
    forward = jnp.stack([jnp.cos(angle) * scale, -jnp.sin(angle) * scale], axis=1).astype(
        jnp.bfloat16
    )
    inverse = jnp.stack([jnp.cos(angle), -jnp.sin(angle)], axis=1).astype(jnp.bfloat16)
    return (forward, inverse)


def taper_weights(aperture, taper_level, surface_points):
    ends = aperture * BLOCK
    ramp = jnp.minimum(TAPER * (1 + taper_level), ends)
    begins = ends - ramp
    offset = (surface_points - begins + 1).astype(jnp.float32)
    wave = jnp.cos(0.5 * math.pi * offset / (ramp + 1).astype(jnp.float32))
    inside = jnp.where(surface_points < ends, wave * wave, jnp.zeros_like(wave))
    return jnp.where(surface_points < begins, jnp.ones_like(wave), inside)


def body(shot_gathers, aperture_blocks, taper_index):
    time_local, rows_local, points_total = shot_gathers.shape
    owners = lax.axis_size("freq")
    slot_count = 2 * F_DEV
    time_total = time_local * owners
    freq_total = F_DEV * owners
    owner_index = lax.axis_index("freq")
    panel_index = lax.axis_index("panel")
    owner_range = jnp.arange(owners, dtype=jnp.int32)
    freq_range = jnp.arange(freq_total, dtype=jnp.int32)
    assignment = freq_range.reshape(owners, F_DEV)
    forward, inverse = transform_tables(freq_total, time_total)
    selector = (assignment.reshape(-1)[:, None] == freq_range[None, :]).astype(jnp.bfloat16)
    picked_forward = jnp.dot(
        selector, forward.reshape(freq_total, 2 * time_total), preferred_element_type=jnp.float32
    ).astype(jnp.bfloat16)
    forward_rows = (
        picked_forward.reshape(owners, F_DEV, 2, time_total)
        .transpose(1, 2, 0, 3)
        .reshape(slot_count, owners, time_total)
    )
    picked_inverse = jnp.dot(
        selector, inverse.reshape(freq_total, 2 * time_total), preferred_element_type=jnp.float32
    ).astype(jnp.bfloat16)
    inverse_rows = picked_inverse.reshape(owners * slot_count, owners, time_local)
    trace_width = rows_local * points_total // owners
    outgoing_time = shot_gathers.reshape(time_local, owners, trace_width)
    series = lax.all_to_all(outgoing_time, "freq", split_axis=1, concat_axis=0, tiled=True)[:, 0, :]
    spectra = jnp.einsum(
        "qot,tw->qow", forward_rows, series, preferred_element_type=jnp.float32
    ).astype(jnp.bfloat16)
    own_spectra = lax.all_to_all(spectra, "freq", split_axis=1, concat_axis=1, tiled=True)
    own_spectra = own_spectra.reshape(F_DEV, 2, rows_local, points_total)
    mine = owner_range[:, None] == owner_index
    my_freqs = jnp.sum(jnp.where(mine, assignment, jnp.zeros_like(assignment)), axis=0)
    matches = my_freqs[:, None] == freq_range[None, :]
    my_aperture = jnp.sum(jnp.where(matches, aperture_blocks[None, :], 0), axis=1)
    my_taper = jnp.sum(jnp.where(matches, taper_index[None, :], 0), axis=1)
    local_points = panel_index * rows_local + jnp.arange(rows_local, dtype=jnp.int32)
    weights = taper_weights(my_aperture[:, None], my_taper[:, None], local_points[None, :])
    tapered = (weights[:, None, :, None] * own_spectra[:, :, :, :SW].astype(jnp.float32)).astype(
        jnp.bfloat16
    )
    piece = lax.all_gather(tapered, "panel", axis=2, tiled=True)
    updated_list = []
    for slot_index in range(F_DEV):
        left_block = own_spectra[slot_index]
        stacked_left = jnp.concatenate([left_block[0], left_block[1]], axis=1)
        real_side = jnp.concatenate([piece[slot_index, 0], -piece[slot_index, 1]], axis=0)
        imag_side = jnp.concatenate([piece[slot_index, 1], piece[slot_index, 0]], axis=0)
        stacked_right = jnp.stack([real_side, imag_side], axis=0)
        updated = jnp.einsum(
            "rk,cks->crs", stacked_left, stacked_right, preferred_element_type=jnp.float32
        )
        updated_list.append(updated)
    summed = jnp.stack(updated_list, axis=0)
    multiples = (summed * (-1.0 / math.sqrt(points_total))).astype(jnp.bfloat16)
    output_width = rows_local * SW // owners
    outgoing_freq = multiples.reshape(slot_count, owners, output_width)
    output_scale = 1.0 / math.sqrt(freq_total)
    values = lax.all_to_all(outgoing_freq, "freq", split_axis=1, concat_axis=0, tiled=True)[:, 0, :]
    traces = (
        jnp.einsum("qgt,qw->tgw", inverse_rows, values, preferred_element_type=jnp.float32)
        * output_scale
    )
    result = lax.all_to_all(
        traces.astype(jnp.bfloat16), "freq", split_axis=1, concat_axis=1, tiled=True
    )
    return result.reshape(time_local, rows_local, SW)


def solution(mesh):
    return jax.shard_map(
        body,
        mesh=mesh,
        in_specs=(P("freq", "panel", None), P(), P()),
        out_specs=P("freq", "panel", None),
        check_vma=False,
    )
```

profile of v0, /device:TPU:0, one launch (start us, length us, event | category | flops | bytes accessed | tf_op | source)
XLA Modules:
  0.0 1098.2 jit_solution(10738489167989122141)
XLA Ops:
  6.5 17.0 %reshape.339 = bf16[4,16,131072]{2,1,0:T(8,128)(2,1)} reshape(bf16[4,1024,2048]{2,1,0:T(8,128)(2,1)} %param.3) | data formatting | bytes 33554432 | tf_op jit(solution)/shard_map/reshape | solution.py:62
  23.5 22.1 %copy.53 = bf16[4,16,131072]{2,0,1:T(4,128)(2,1)} copy(bf16[4,16,131072]{2,1,0:T(8,128)(2,1)} %reshape.339) | data formatting | bytes 33554432 | tf_op jit(solution)/shard_map/reshape | solution.py:62
  45.6 8.4 all-to-all-start
  54.0 0.2 fusion.29
  54.2 0.1 convert_element_type.85
  54.3 0.1 convolution_convert_fusion.2
  54.4 0.1 reshape.337
  54.5 314.8 %all-to-all-done = bf16[4,16,131072]{2,0,1:T(4,128)(2,1)} async-done(((bf16[4,16,131072]{2,0,1:T(4,128)(2,1)}), bf16[4,16,131072]{2,0,1:T(4,128)(2,1)}, u32[]{:S(2)}, u32[]{:S(2)}) %all-to-all-start) | async-done | bytes 16777248 | tf_op jit(solution)/shard_map/all_to_all | solution.py:63
  369.3 15.0 %reshape.343 = bf16[64,131072,1]{1,0,2:T(8,128)(2,1)} reshape(bf16[16,4,1,131072]{3,1,0,2:T(4,128)(2,1)} %bitcast.3) | data formatting | bytes 33554432 | tf_op jit(solution)/shard_map/squeeze | solution.py:63
  384.4 11.4 %convolution_convert_fusion = bf16[4,16,131072]{2,1,0:T(8,128)(2,1)} fusion(bf16[4,16,64]{2,1,0:T(8,128)(2,1)S(1)} %bitcast.61, bf16[64,131072,1]{1,0,2:T(8,128)(2,1)} %reshape.343), kind=kOutput, calls=%fused_computation | convolution fusion | flops 1082130432 | bytes 33562624 | tf_op jit(solution)/shard_map/qot,tw->qow/dot_general | solution.py:64
  395.8 22.1 %copy.54 = bf16[4,16,131072]{2,0,1:T(4,128)(2,1)} copy(bf16[4,16,131072]{2,1,0:T(8,128)(2,1)} %convolution_convert_fusion) | data formatting | bytes 33554432 | tf_op jit(solution)/shard_map/convert_element_type | solution.py:66
  417.9 0.0 copy-start.4
  417.9 0.0 copy-start.5
  417.9 73.2 %all-to-all-start.1 = ((bf16[4,16,131072]{2,0,1:T(4,128)(2,1)}), bf16[4,16,131072]{2,0,1:T(4,128)(2,1)}, u32[]{:S(2)}, u32[]{:S(2)}) async-start(bf16[4,16,131072]{2,0,1:T(4,128)(2,1)} %copy.54), calls=%async_computation.1 | async-start | bytes 33554432 | tf_op jit(solution)/shard_map/all_to_all | solution.py:67
  491.1 0.2 all-gather.2.cloned.1.call-start
  491.4 0.1 select_reduce_fusion.2
  491.5 0.0 copy-done.4
  491.5 0.0 copy-done.5
  491.5 0.2 select_reduce_fusion.1
  491.7 0.2 compare_select_fusion.1
  491.9 311.9 %all-to-all-done.1 = bf16[4,16,131072]{2,0,1:T(4,128)(2,1)} async-done(((bf16[4,16,131072]{2,0,1:T(4,128)(2,1)}), bf16[4,16,131072]{2,0,1:T(4,128)(2,1)}, u32[]{:S(2)}, u32[]{:S(2)}) %all-to-all-start.1) | async-done | bytes 16777248 | tf_op jit(solution)/shard_map/all_to_all | solution.py:67
  803.8 18.5 %copy.55 = bf16[4,16,131072]{2,1,0:T(8,128)(2,1)} copy(bf16[4,16,131072]{2,0,1:T(4,128)(2,1)} %all-to-all-done.1) | data formatting | bytes 33554432 | tf_op jit(solution)/shard_map/all_to_all | solution.py:67
  822.3 17.0 %reshape.340 = bf16[2,2,1024,2048]{3,2,1,0:T(8,128)(2,1)} reshape(bf16[4,16,131072]{2,1,0:T(8,128)(2,1)} %copy.55) | data formatting | bytes 33554432 | tf_op jit(solution)/shard_map/reshape | solution.py:68
  839.3 1.3 slice.52
  840.6 0.5 copy.63
  841.2 1.2 multiply_convert_fusion
  842.4 0.0 all-gather.2.cloned.1.call-update
  842.4 86.1 %slice_reduce_fusion.3 = (bf16[16,131072]{1,0:T(8,128)(2,1)}, bf16[16,131072]{1,0:T(8,128)(2,1)}, bf16[16,131072]{1,0:T(8,128)(2,1)}, bf16[16,131072]{1,0:T(8,128)(2,1)}) fusion(bf16[4,16,131072]{2,0,1:T(4,128)(2,1)} %all-to-all-done.1), kind=kLoop, calls=%fused_computation.7 | loop fusion | bytes 33554432 | tf_op jit(solution)/shard_map/slice | solution.py:83
  928.5 4.8 squeeze.44
  933.3 4.8 squeeze.43
  938.1 4.8 squeeze.40
  942.9 4.8 squeeze.39
  947.8 0.0 all-gather.2.cloned.1.call-done
  947.8 1.3 fusion.33
  949.0 0.0 copy-start.3
  949.0 1.8 slice_bitcast_fusion.2
  950.8 0.0 copy-start.1
  950.9 0.2 maximum_bitcast_fusion.10
  951.1 0.2 maximum_bitcast_fusion.8
  951.3 0.5 copy-done.3
  951.8 1.5 copy-done.1
  953.4 0.0 copy-start
  953.4 0.0 copy-start.2
  953.4 2.4 fusion.15
  955.7 0.0 copy-done
  955.7 1.1 copy-done.2
  956.8 2.4 fusion.18
  959.2 0.3 fusion.14
  959.5 0.7 copy.57
  960.1 0.8 convert_element_type.91
  960.9 1.8 copy.58
  962.7 72.7 %all-to-all-start.2 = ((bf16[4,16,8192]{2,0,1:T(4,128)(2,1)}), bf16[4,16,8192]{2,0,1:T(4,128)(2,1)S(1)}, u32[]{:S(2)}, u32[]{:S(2)}) async-start(bf16[4,16,8192]{2,0,1:T(4,128)(2,1)} %copy.58), calls=%async_computation.2 | async-start | bytes 2097152 | tf_op jit(solution)/shard_map/all_to_all | solution.py:96
  1035.4 0.1 convert_element_type.92
  1035.5 0.1 convolution_convert_fusion.1
  1035.6 0.6 reshape.341
  1036.2 0.3 copy.60
  1036.5 21.5 %all-to-all-done.2 = bf16[4,16,8192]{2,0,1:T(4,128)(2,1)S(1)} async-done(((bf16[4,16,8192]{2,0,1:T(4,128)(2,1)}), bf16[4,16,8192]{2,0,1:T(4,128)(2,1)S(1)}, u32[]{:S(2)}, u32[]{:S(2)}) %all-to-all-start.2) | async-done | bytes 1048608 | tf_op jit(solution)/shard_map/all_to_all | solution.py:96
  1057.9 0.3 reshape.346
  1058.2 0.4 fusion.1
  1058.6 0.8 copy.61
  1059.5 30.0 %all_to_all.40 = bf16[4,16,8192]{2,0,1:T(4,128)(2,1)S(1)} all-to-all(bf16[4,16,8192]{2,0,1:T(4,128)(2,1)S(1)} %copy.61), channel_id=1, replica_groups=mesh['freq'=16,'panel'=2] {'freq'}, dimensions={1} | all-to-all | bytes 2097152 | tf_op jit(solution)/shard_map/all_to_all | solution.py:101
  1089.5 0.6 copy.62
  1090.1 1.3 reshape.342
  (8 shorter events, 0.1 us)
Async XLA Ops:
  45.6 323.7 %all-to-all-start = ((bf16[4,16,131072]{2,0,1:T(4,128)(2,1)}), bf16[4,16,131072]{2,0,1:T(4,128)(2,1)}, u32[]{:S(2)}, u32[]{:S(2)}) async-start(bf16[4,16,131072]{2,0,1:T(4,128)(2,1)} %copy.53), calls=%async_computation | async-start | bytes 33554432 | tf_op jit(solution)/shard_map/all_to_all | solution.py:63
  417.9 73.6 %copy-start.4 = (s32[32]{0:T(128)S(1)}, s32[32]{0:T(128)}, u32[]{:S(2)}) copy-start(s32[32]{0:T(128)} %param.4) | copy-start | bytes 388
  417.9 73.6 %copy-start.5 = (s32[32]{0:T(128)S(1)}, s32[32]{0:T(128)}, u32[]{:S(2)}) copy-start(s32[32]{0:T(128)} %param.5) | copy-start | bytes 388
  417.9 385.9 %all-to-all-start.1 = ((bf16[4,16,131072]{2,0,1:T(4,128)(2,1)}), bf16[4,16,131072]{2,0,1:T(4,128)(2,1)}, u32[]{:S(2)}, u32[]{:S(2)}) async-start(bf16[4,16,131072]{2,0,1:T(4,128)(2,1)} %copy.54), calls=%async_computation.1 | async-start | bytes 33554432 | tf_op jit(solution)/shard_map/all_to_all | solution.py:67
  491.1 456.6 %all-gather.2.cloned.1.call-start = ((), (), s32[]{:S(2)}) async-start(), calls=%async_computation.4 | async-start | bytes 3145728 | tf_op jit(solution)/shard_map/all_gather | solution.py:79
  949.0 2.8 copy-start.3
  950.8 2.5 copy-start.1
  953.4 2.4 copy-start
  953.4 3.5 copy-start.2
  962.7 95.3 %all-to-all-start.2 = ((bf16[4,16,8192]{2,0,1:T(4,128)(2,1)}), bf16[4,16,8192]{2,0,1:T(4,128)(2,1)S(1)}, u32[]{:S(2)}, u32[]{:S(2)}) async-start(bf16[4,16,8192]{2,0,1:T(4,128)(2,1)} %copy.58), calls=%async_computation.2 | async-start | bytes 2097152 | tf_op jit(solution)/shard_map/all_to_all | solution.py:96
Sparse Core Ops, SparseCore 0:
  842.5 77.6 all-gather.1
where the time goes:
time: 1100 us
  waiting for transfers between devices  648 us (59%)
  local copies, waits for them, and re-layouts  231 us (21%)
  starting transfers between devices  154 us (14%)
  blocking collectives  30 us (3%)
  matrix products  16.8 us (2%)
  between operations  13.6 us (1%)
    all_to_all x1, waiting for transfers between devices, body(): lax.all_to_all(outgoing_time, 'freq', split_axis=1, concat_axis=0, tiled=...  315 us
    all_to_all x1, waiting for transfers between devices, body(): lax.all_to_all(spectra, 'freq', split_axis=1, concat_axis=1, tiled=True)  312 us
    slice x1, local copies, waits for them, and re-layouts, body(): stacked_left = jnp.concatenate([left_block[0], left_block[1]], axis=1)  86.1 us
    all_to_all x1, starting transfers between devices, body(): lax.all_to_all(spectra, 'freq', split_axis=1, concat_axis=1, tiled=True)  73.2 us
    all_to_all x1, starting transfers between devices, body(): lax.all_to_all(outgoing_freq, 'freq', split_axis=1, concat_axis=0, tiled=...  72.7 us
    reshape x2, local copies, waits for them, and re-layouts, body(): outgoing_time = shot_gathers.reshape(time_local, owners, trace_width)  39.1 us
    all_to_all x1, blocking collectives, body(): lax.all_to_all(traces.astype(jnp.bfloat16), 'freq', split_axis=1, concat_...  30 us
    convert_element_type x1, local copies, waits for them, and re-layouts, body(): spectra = jnp.einsum('qot,tw->qow', forward_rows, series, preferred_eleme...  22.1 us
  transfers between devices with their start and end apart: 4, of which 3 were waited for; matrix products, arithmetic and copies ran while one was open for 10% of the time, Pallas kernels for 0%

commit v1 on v0

--- a/solution.py
+++ b/solution.py
@@ -98,9 +98,20 @@
         jnp.einsum("qgt,qw->tgw", inverse_rows, values, preferred_element_type=jnp.float32)
         * output_scale
     )
-    result = lax.all_to_all(
-        traces.astype(jnp.bfloat16), "freq", split_axis=1, concat_axis=1, tiled=True
-    )
+    value = traces.astype(jnp.bfloat16)
+    ways, here = (lax.axis_size("freq"), lax.axis_index("freq"))
+    width = value.shape[1] // ways
+    shape = list(value.shape)
+    shape[1] = width
+    height = shape[1]
+    shape[1] = height * ways
+    full = jnp.zeros(shape, value.dtype)
+    for mask in range(ways):
+        part = lax.dynamic_slice_in_dim(value, (here ^ mask) * width, width, axis=1)
+        if mask:
+            part = lax.ppermute(part, "freq", [(d, d ^ mask) for d in range(ways)])
+        full = lax.dynamic_update_slice_in_dim(full, part, (here ^ mask) * height, axis=1)
+    result = full
     return result.reshape(time_local, rows_local, SW)
 
 

time: 1100 us -> 1160 us (1.055)
  local copies, waits for them, and re-layouts: 231 us -> 268 us
  blocking collectives: 30 us -> 0 us
  starting transfers between devices: 154 us -> 181 us
  waiting for transfers between devices: 648 us -> 668 us
    dynamic_update_slice x0 -> x16, local copies, waits for them, and re-layouts: none -> 34 us  [body(): lax.dynamic_update_slice_in_dim(full, part, (here ^ mask) * height, axis=1)]
    all_to_all x1 -> x0, blocking collectives: 30 us -> none  [body(): lax.all_to_all(traces.astype(jnp.bfloat16), 'freq', split_axis=1, concat_...]
    ppermute x0 -> x15, starting transfers between devices: none -> 25.9 us  [body(): part = lax.ppermute(part, 'freq', [(d, d ^ mask) for d in range(ways)])]
    ppermute x0 -> x15, waiting for transfers between devices: none -> 20.4 us  [body(): part = lax.ppermute(part, 'freq', [(d, d ^ mask) for d in range(ways)])]
  transfers between devices with their start and end apart: 4 -> 19, of which waited for: 3 -> 8; matrix products, arithmetic and copies ran while one was open for 10% -> 12% of each run, Pallas kernels for 0% -> 0%
where the time goes in v1:
time: 1160 us; the launch traced here: 1150 us
  waiting for transfers between devices  668 us (58%)
  local copies, waits for them, and re-layouts  268 us (23%)
  starting transfers between devices  181 us (16%)
  matrix products  16.8 us (1%)
  between operations  14.2 us (1%)
    all_to_all x1, waiting for transfers between devices, body(): lax.all_to_all(outgoing_time, 'freq', split_axis=1, concat_axis=0, tiled=...  315 us
    all_to_all x1, waiting for transfers between devices, body(): lax.all_to_all(spectra, 'freq', split_axis=1, concat_axis=1, tiled=True)  312 us
    slice x1, local copies, waits for them, and re-layouts, body(): stacked_left = jnp.concatenate([left_block[0], left_block[1]], axis=1)  86 us
    all_to_all x1, starting transfers between devices, body(): lax.all_to_all(spectra, 'freq', split_axis=1, concat_axis=1, tiled=True)  73.2 us
    all_to_all x1, starting transfers between devices, body(): lax.all_to_all(outgoing_freq, 'freq', split_axis=1, concat_axis=0, tiled=...  72.7 us
    reshape x2, local copies, waits for them, and re-layouts, body(): outgoing_time = shot_gathers.reshape(time_local, owners, trace_width)  39.1 us
    dynamic_update_slice x16, local copies, waits for them, and re-layouts, body(): lax.dynamic_update_slice_in_dim(full, part, (here ^ mask) * height, axis=1)  34 us
    ppermute x15, starting transfers between devices, body(): part = lax.ppermute(part, 'freq', [(d, d ^ mask) for d in range(ways)])  25.9 us
  transfers between devices with their start and end apart: 19, of which 8 were waited for; matrix products, arithmetic and copies ran while one was open for 12% of the time, Pallas kernels for 0%

profile of v1, /device:TPU:0, one launch (start us, length us, event | category | flops | bytes accessed | tf_op | source)
XLA Modules:
  0.0 1150.7 jit_solution(17960798767083741591)
XLA Ops:
  6.5 17.0 %reshape.339 = bf16[4,16,131072]{2,1,0:T(8,128)(2,1)} reshape(bf16[4,1024,2048]{2,1,0:T(8,128)(2,1)} %param.3) | data formatting | bytes 33554432 | tf_op jit(solution)/shard_map/reshape | solution.py:62
  23.5 22.2 %copy.46 = bf16[4,16,131072]{2,0,1:T(4,128)(2,1)} copy(bf16[4,16,131072]{2,1,0:T(8,128)(2,1)} %reshape.339) | data formatting | bytes 33554432 | tf_op jit(solution)/shard_map/reshape | solution.py:62
  45.7 8.4 all-to-all-start
  54.6 314.8 %all-to-all-done = bf16[4,16,131072]{2,0,1:T(4,128)(2,1)} async-done(((bf16[4,16,131072]{2,0,1:T(4,128)(2,1)}), bf16[4,16,131072]{2,0,1:T(4,128)(2,1)}, u32[]{:S(2)}, u32[]{:S(2)}) %all-to-all-start) | async-done | bytes 16777248 | tf_op jit(solution)/shard_map/all_to_all | solution.py:63
  369.4 15.0 %reshape.343 = bf16[64,131072,1]{1,0,2:T(8,128)(2,1)} reshape(bf16[16,4,1,131072]{3,1,0,2:T(4,128)(2,1)} %bitcast.3) | data formatting | bytes 33554432 | tf_op jit(solution)/shard_map/squeeze | solution.py:63
  384.4 11.4 convolution_convert_fusion
  395.9 22.2 %copy.47 = bf16[4,16,131072]{2,0,1:T(4,128)(2,1)} copy(bf16[4,16,131072]{2,1,0:T(8,128)(2,1)} %convolution_convert_fusion) | data formatting | bytes 33554432 | tf_op jit(solution)/shard_map/convert_element_type | solution.py:66
  418.0 73.2 %all-to-all-start.1 = ((bf16[4,16,131072]{2,0,1:T(4,128)(2,1)}), bf16[4,16,131072]{2,0,1:T(4,128)(2,1)}, u32[]{:S(2)}, u32[]{:S(2)}) async-start(bf16[4,16,131072]{2,0,1:T(4,128)(2,1)} %copy.47), calls=%async_computation.1 | async-start | bytes 33554432 | tf_op jit(solution)/shard_map/all_to_all | solution.py:67
  492.3 311.6 %all-to-all-done.1 = bf16[4,16,131072]{2,0,1:T(4,128)(2,1)} async-done(((bf16[4,16,131072]{2,0,1:T(4,128)(2,1)}), bf16[4,16,131072]{2,0,1:T(4,128)(2,1)}, u32[]{:S(2)}, u32[]{:S(2)}) %all-to-all-start.1) | async-done | bytes 16777248 | tf_op jit(solution)/shard_map/all_to_all | solution.py:67
  804.0 18.6 %copy.48 = bf16[4,16,131072]{2,1,0:T(8,128)(2,1)} copy(bf16[4,16,131072]{2,0,1:T(4,128)(2,1)} %all-to-all-done.1) | data formatting | bytes 33554432 | tf_op jit(solution)/shard_map/all_to_all | solution.py:67
  822.6 17.0 %reshape.340 = bf16[2,2,1024,2048]{3,2,1,0:T(8,128)(2,1)} reshape(bf16[4,16,131072]{2,1,0:T(8,128)(2,1)} %copy.48) | data formatting | bytes 33554432 | tf_op jit(solution)/shard_map/reshape | solution.py:68
  839.5 1.3 slice.52
  841.4 1.2 multiply_convert_fusion
  842.6 86.0 %slice_reduce_fusion.3 = (bf16[16,131072]{1,0:T(8,128)(2,1)}, bf16[16,131072]{1,0:T(8,128)(2,1)}, bf16[16,131072]{1,0:T(8,128)(2,1)}, bf16[16,131072]{1,0:T(8,128)(2,1)}) fusion(bf16[4,16,131072]{2,0,1:T(4,128)(2,1)} %all-to-all-done.1), kind=kLoop, calls=%fused_computation.6 | loop fusion | bytes 33554432 | tf_op jit(solution)/shard_map/slice | solution.py:83
  928.7 4.8 squeeze.39
  933.5 4.8 squeeze.40
  938.3 4.9 squeeze.43
  943.2 4.8 squeeze.44
  948.0 1.8 slice_bitcast_fusion.2
  950.7 1.7 copy-done.4
  952.4 1.3 copy-done.2
  953.7 2.4 fusion.17
  956.0 1.1 copy-done.3
  957.1 2.4 fusion.14
  959.8 0.7 copy.50
  960.4 0.7 convert_element_type.89
  961.2 1.8 copy.51
  962.9 72.7 %all-to-all-start.2 = ((bf16[4,16,8192]{2,0,1:T(4,128)(2,1)}), bf16[4,16,8192]{2,0,1:T(4,128)(2,1)S(1)}, u32[]{:S(2)}, u32[]{:S(2)}) async-start(bf16[4,16,8192]{2,0,1:T(4,128)(2,1)} %copy.51), calls=%async_computation.2 | async-start | bytes 2097152 | tf_op jit(solution)/shard_map/all_to_all | solution.py:96
  1036.8 21.4 %all-to-all-done.2 = bf16[4,16,8192]{2,0,1:T(4,128)(2,1)S(1)} async-done(((bf16[4,16,8192]{2,0,1:T(4,128)(2,1)}), bf16[4,16,8192]{2,0,1:T(4,128)(2,1)S(1)}, u32[]{:S(2)}, u32[]{:S(2)}) %all-to-all-start.2) | async-done | bytes 1048608 | tf_op jit(solution)/shard_map/all_to_all | solution.py:96
  1058.9 2.8 dynamic-slice_bitcast_fusion
  1062.3 1.7 collective-permute-start.1
  1064.0 1.2 collective-permute-start.2
  1065.2 2.5 collective-permute-start.3
  1067.7 4.1 collective-permute-start.5
  1071.8 3.0 collective-permute-start.7
  1074.8 0.9 collective-permute-start.8
  1075.6 3.5 collective-permute-done.4
  1079.1 0.7 collective-permute-start.9
  1079.8 2.7 collective-permute-done.5
  1082.5 0.8 collective-permute-start.10
  1083.3 1.5 collective-permute-done.6
  1084.8 1.6 collective-permute-start.11
  1086.4 10.7 collective-permute-done.7
  1097.1 1.6 collective-permute-start.12
  1098.7 2.0 collective-permute-done.8
  1100.7 3.1 collective-permute-start.13
  1103.9 4.2 collective-permute-start.14
  1108.1 2.0 dynamic_update_slice.48
  1110.1 2.0 dynamic_update_slice.49
  1112.1 2.0 dynamic_update_slice.50
  1114.1 2.0 dynamic_update_slice.51
  1116.1 2.0 dynamic_update_slice.52
  1118.2 2.0 dynamic_update_slice.53
  1120.2 2.0 dynamic_update_slice.54
  1122.2 2.0 dynamic_update_slice.55
  1124.2 2.0 dynamic_update_slice.56
  1126.2 2.0 dynamic_update_slice.57
  1128.2 2.0 dynamic_update_slice.58
  1130.2 2.0 dynamic_update_slice.59
  1132.2 2.0 dynamic_update_slice.60
  1134.2 3.0 dynamic_update_slice.61
  1137.3 3.0 dynamic_update_slice.62
  1140.3 2.0 dynamic_update_slice.63
  1142.3 1.3 reshape.342
  (54 shorter events, 5.8 us)
Async XLA Ops:
  45.7 323.7 %all-to-all-start = ((bf16[4,16,131072]{2,0,1:T(4,128)(2,1)}), bf16[4,16,131072]{2,0,1:T(4,128)(2,1)}, u32[]{:S(2)}, u32[]{:S(2)}) async-start(bf16[4,16,131072]{2,0,1:T(4,128)(2,1)} %copy.46), calls=%async_computation | async-start | bytes 33554432 | tf_op jit(solution)/shard_map/all_to_all | solution.py:63
  418.0 73.9 %copy-start.5 = (s32[32]{0:T(128)S(1)}, s32[32]{0:T(128)}, u32[]{:S(2)}) copy-start(s32[32]{0:T(128)} %param.4) | copy-start | bytes 388
  418.0 73.9 %copy-start.6 = (s32[32]{0:T(128)S(1)}, s32[32]{0:T(128)}, u32[]{:S(2)}) copy-start(s32[32]{0:T(128)} %param.5) | copy-start | bytes 388
  418.0 385.9 %all-to-all-start.1 = ((bf16[4,16,131072]{2,0,1:T(4,128)(2,1)}), bf16[4,16,131072]{2,0,1:T(4,128)(2,1)}, u32[]{:S(2)}, u32[]{:S(2)}) async-start(bf16[4,16,131072]{2,0,1:T(4,128)(2,1)} %copy.47), calls=%async_computation.1 | async-start | bytes 33554432 | tf_op jit(solution)/shard_map/all_to_all | solution.py:67
  491.3 456.7 %all-gather.2.cloned.1.call-start = ((), (), s32[]{:S(2)}) async-start(), calls=%async_computation.3 | async-start | bytes 3145728 | tf_op jit(solution)/shard_map/all_gather | solution.py:79
  948.0 2.2 copy-start
  950.2 2.2 copy-start.4
  950.3 3.4 copy-start.2
  953.7 2.4 copy-start.1
  953.7 3.5 copy-start.3
  962.9 95.3 %all-to-all-start.2 = ((bf16[4,16,8192]{2,0,1:T(4,128)(2,1)}), bf16[4,16,8192]{2,0,1:T(4,128)(2,1)S(1)}, u32[]{:S(2)}, u32[]{:S(2)}) async-start(bf16[4,16,8192]{2,0,1:T(4,128)(2,1)} %copy.51), calls=%async_computation.2 | async-start | bytes 2097152 | tf_op jit(solution)/shard_map/all_to_all | solution.py:96
  1061.7 6.0 collective-permute-start
  1062.3 9.5 collective-permute-start.1
  1064.0 7.8 collective-permute-start.2
  1065.2 9.6 collective-permute-start.3
  1067.7 11.4 collective-permute-start.4
  1067.7 14.8 %collective-permute-start.5 = (bf16[4,1,8192]{2,1,0:T(2,128)(2,1)S(1)}, bf16[4,1,8192]{2,1,0:T(2,128)(2,1)S(1)}, u32[]{:S(2)}, u32[]{:S(2)}) collective-permute-start(bf16[4,1,8192]{2,1,0:T(2,128)(2,1)S(1)} %get-tuple-element.26), channel_id=1, source_target_pairs={{0,12},{2,14},{4,8},{6,10},{8,4},{10,6},{12,0},{14,2},{16,28},{18,... | collective-permute-start | bytes 196616 | tf_op jit(solution)/shard_map/ppermute | solution.py:112
  1071.8 13.0 %collective-permute-start.6 = (bf16[4,1,8192]{2,1,0:T(2,128)(2,1)S(1)}, bf16[4,1,8192]{2,1,0:T(2,128)(2,1)S(1)}, u32[]{:S(2)}, u32[]{:S(2)}) collective-permute-start(bf16[4,1,8192]{2,1,0:T(2,128)(2,1)S(1)} %get-tuple-element.25), channel_id=1, source_target_pairs={{0,14},{2,12},{4,10},{6,8},{8,6},{10,4},{12,2},{14,0},{16,30},{18,... | collective-permute-start | bytes 196616 | tf_op jit(solution)/shard_map/ppermute | solution.py:112
  1071.8 25.3 %collective-permute-start.7 = (bf16[4,1,8192]{2,1,0:T(2,128)(2,1)S(1)}, bf16[4,1,8192]{2,1,0:T(2,128)(2,1)S(1)}, u32[]{:S(2)}, u32[]{:S(2)}) collective-permute-start(bf16[4,1,8192]{2,1,0:T(2,128)(2,1)S(1)} %get-tuple-element.24), channel_id=1, source_target_pairs={{0,16},{2,18},{4,20},{6,22},{8,24},{10,26},{12,28},{14,30},{16,0},... | collective-permute-start | bytes 196616 | tf_op jit(solution)/shard_map/ppermute | solution.py:112
  1074.8 26.0 %collective-permute-start.8 = (bf16[4,1,8192]{2,1,0:T(2,128)(2,1)S(1)}, bf16[4,1,8192]{2,1,0:T(2,128)(2,1)S(1)}, u32[]{:S(2)}, u32[]{:S(2)}) collective-permute-start(bf16[4,1,8192]{2,1,0:T(2,128)(2,1)S(1)} %get-tuple-element.23), channel_id=1, source_target_pairs={{0,18},{2,16},{4,22},{6,20},{8,26},{10,24},{12,30},{14,28},{16,2},... | collective-permute-start | bytes 196616 | tf_op jit(solution)/shard_map/ppermute | solution.py:112
  1079.1 24.8 %collective-permute-start.9 = (bf16[4,1,8192]{2,1,0:T(2,128)(2,1)S(1)}, bf16[4,1,8192]{2,1,0:T(2,128)(2,1)S(1)}, u32[]{:S(2)}, u32[]{:S(2)}) collective-permute-start(bf16[4,1,8192]{2,1,0:T(2,128)(2,1)S(1)} %get-tuple-element.22), channel_id=1, source_target_pairs={{0,20},{2,22},{4,16},{6,18},{8,28},{10,30},{12,24},{14,26},{16,4},... | collective-permute-start | bytes 196616 | tf_op jit(solution)/shard_map/ppermute | solution.py:112
  1082.5 47.7 %collective-permute-start.10 = (bf16[4,1,8192]{2,1,0:T(2,128)(2,1)S(1)}, bf16[4,1,8192]{2,1,0:T(2,128)(2,1)S(1)}, u32[]{:S(2)}, u32[]{:S(2)}) collective-permute-start(bf16[4,1,8192]{2,1,0:T(2,128)(2,1)S(1)} %get-tuple-element.21), channel_id=1, source_target_pairs={{0,22},{2,20},{4,18},{6,16},{8,30},{10,28},{12,26},{14,24},{16,6},... | collective-permute-start | bytes 196616 | tf_op jit(solution)/shard_map/ppermute | solution.py:112
  1084.8 47.4 %collective-permute-start.11 = (bf16[4,1,8192]{2,1,0:T(2,128)(2,1)S(1)}, bf16[4,1,8192]{2,1,0:T(2,128)(2,1)S(1)}, u32[]{:S(2)}, u32[]{:S(2)}) collective-permute-start(bf16[4,1,8192]{2,1,0:T(2,128)(2,1)S(1)} %get-tuple-element.20), channel_id=1, source_target_pairs={{0,24},{2,26},{4,28},{6,30},{8,16},{10,18},{12,20},{14,22},{16,8},... | collective-permute-start | bytes 196616 | tf_op jit(solution)/shard_map/ppermute | solution.py:112
  1097.1 37.1 %collective-permute-start.12 = (bf16[4,1,8192]{2,1,0:T(2,128)(2,1)S(1)}, bf16[4,1,8192]{2,1,0:T(2,128)(2,1)}, u32[]{:S(2)}, u32[]{:S(2)}) collective-permute-start(bf16[4,1,8192]{2,1,0:T(2,128)(2,1)S(1)} %get-tuple-element.19), channel_id=1, source_target_pairs={{0,26},{2,24},{4,30},{6,28},{8,18},{10,16},{12,22},{14,20},{16,10}... | collective-permute-start | bytes 196616 | tf_op jit(solution)/shard_map/ppermute | solution.py:112
  1100.7 36.5 %collective-permute-start.13 = (bf16[4,1,8192]{2,1,0:T(2,128)(2,1)S(1)}, bf16[4,1,8192]{2,1,0:T(2,128)(2,1)}, u32[]{:S(2)}, u32[]{:S(2)}) collective-permute-start(bf16[4,1,8192]{2,1,0:T(2,128)(2,1)S(1)} %get-tuple-element.18), channel_id=1, source_target_pairs={{0,28},{2,30},{4,24},{6,26},{8,20},{10,22},{12,16},{14,18},{16,12}... | collective-permute-start | bytes 196616 | tf_op jit(solution)/shard_map/ppermute | solution.py:112
  1103.9 36.4 %collective-permute-start.14 = (bf16[4,1,8192]{2,1,0:T(2,128)(2,1)S(1)}, bf16[4,1,8192]{2,1,0:T(2,128)(2,1)S(1)}, u32[]{:S(2)}, u32[]{:S(2)}) collective-permute-start(bf16[4,1,8192]{2,1,0:T(2,128)(2,1)S(1)} %get-tuple-element.17), channel_id=1, source_target_pairs={{0,30},{2,28},{4,26},{6,24},{8,22},{10,20},{12,18},{14,16},{16,14}... | collective-permute-start | bytes 196616 | tf_op jit(solution)/shard_map/ppermute | solution.py:112
Sparse Core Ops, SparseCore 0:
  842.8 77.6 all-gather.1
